TPU v7x, 32 devices: a whole 2x2x4 slice. The times are simulated.
32 devices in a mesh: dp: 8 (over z, y), mp: 4 (over x, core).
Axes of the slice: x: 2, y: 2, z: 4, core: 2. Of those that a mesh axis runs over, the one named last changes fastest.
Arguments:
- entity_table: float32 [65536, 400], P(('dp', 'mp'))
- entity_rows: float32 [65536], P(('dp', 'mp')), may hold values from 2.0954758e-13 to 8.381903e-13
- entity_cols: float32 [400], replicated, may hold values from 2.0954758e-13 to 8.381903e-13
- relation_table: float32 [2, 25088, 400], P(None, ('dp', 'mp')), may hold values from -0.21 to 0.21
- relation_rows: float32 [2, 25088], P(None, ('dp', 'mp')), may hold values from 1.824632e-13 to 7.298528e-13
- relation_cols: float32 [2, 400], replicated, may hold values from 1.824632e-13 to 7.298528e-13
- requests: int32 [32, 8, 4, 8], P(('dp', 'mp')), may hold values from 0 to 2047
- relation_requests: int32 [32, 8, 4, 8], P(('dp', 'mp')), may hold values from 0 to 783, as said below
- src_slot: int32 [2, 65536], P(None, ('dp', 'mp')), may hold values from 0 to 255
- dst_slot: int32 [2, 65536], P(None, ('dp', 'mp')), may hold values from 0 to 255
- relation_ids: int32 [2, 65536], P(None, ('dp', 'mp')), may hold values from 0 to 255
- edge_valid: int32 [2, 65536], P(None, ('dp', 'mp')), may hold values from 0 to 1, as said below
- neg_slot: int32 [2, 8, 1000], P(None, 'dp', 'mp'), may hold values from 0 to 255
Outputs:
- loss: float32 [2], replicated
- entity_weight: float32 [65536, 400], P(('dp', 'mp'))
- entity_grad: float32 [65536, 400], P(('dp', 'mp'))
- entity_rows_new: float32 [65536], P(('dp', 'mp'))
- entity_cols_new: float32 [400], replicated
- entity_copy: bfloat16 [65536, 400], P(('dp', 'mp'))
- relation_weight: float32 [2, 25088, 400], P(None, ('dp', 'mp'))
- relation_grad: float32 [2, 25088, 400], P(None, ('dp', 'mp'))
- relation_rows_new: float32 [2, 25088], P(None, ('dp', 'mp'))
- relation_cols_new: float32 [2, 400], replicated
- relation_copy: bfloat16 [2, 25088, 400], P(None, ('dp', 'mp'))
Inputs may be any that keep to these rules, and one draw needn't show every extreme that they name: `requests`: a row index within its owner's 2048 rows. `relation_requests`: a relation within its owner's 784 relations; the 8 relations that one device requests from one owner are distinct. `edge_valid`: the share of valid slots rises along the devices.
All inputs are finite; a program needn't handle non-finite values.
Results may differ from a plain program's by a relative error of at most 0.001.
Values sent between devices are 32-bit elements; how exact they have to be, the bound alone decides.
A program may use at most 384 MiB of HBM per device.

v0:
```python
import functools

import jax
import jax.numpy as jnp
from jax import lax
from jax.experimental import pallas as pl
from jax.experimental.pallas import tpu as pltpu
from jax.sharding import PartitionSpec as P

MARGIN = 0.1
EPS_DIST = 1e-06
EPS_SQ = 1e-30
DECAY = 0.5
LEARN = 0.3
CLIP = 0.1
HIGH = lax.Precision.HIGHEST


def score_forward(heads, tails, negative_rows, valid_row):
    offset = heads - tails
    near_dist = jnp.sqrt(jnp.sum(offset * offset, 1) + EPS_DIST)
    cross = jnp.dot(heads, negative_rows.T, precision=HIGH, preferred_element_type=jnp.float32)
    far_dist = jnp.sqrt(
        jnp.sum(heads * heads, 1)[:, None]
        + jnp.sum(negative_rows * negative_rows, 1)[None, :]
        - 2.0 * cross
        + EPS_DIST
    )
    margin_z = MARGIN + near_dist[:, None] - far_dist
    part_sum = jnp.sum(jax.nn.softplus(margin_z) * valid_row[:, None])
    return ((offset, near_dist, far_dist, margin_z), part_sum)


def score_backward(heads, negative_rows, valid_row, kept, pairs):
    offset, near_dist, far_dist, margin_z = kept
    weight = jax.nn.sigmoid(margin_z) * valid_row[:, None] / pairs
    along = weight / far_dist
    pull = jnp.sum(weight, 1) / near_dist
    grad_head = (
        pull[:, None] * offset
        - jnp.sum(along, 1)[:, None] * heads
        + jnp.dot(along, negative_rows, precision=HIGH, preferred_element_type=jnp.float32)
    )
    grad_tail = -pull[:, None] * offset
    return (grad_head, grad_tail, along)


def local_moments(grad, row_moment):
    squares = grad * grad + EPS_SQ
    rows_new = DECAY * row_moment + (1.0 - DECAY) * jnp.mean(squares, 1)
    weighted = jnp.sum(grad * grad / rows_new[:, None], 0)
    return (rows_new, jnp.sum(squares, 0), jnp.sum(rows_new), weighted)


def scaled_update(grad, rows_new, cols_new, row_mean):
    return grad * lax.rsqrt(rows_new[:, None] * cols_new[None, :] / row_mean)


def shards(
    entity_table,
    entity_rows,
    entity_cols,
    relation_table,
    relation_rows,
    relation_cols,
    requests,
    relation_requests,
    src_slot,
    dst_slot,
    relation_ids,
    edge_valid,
    neg_slot,
):
    width = entity_table.shape[1]
    n_data = lax.axis_size("dp")
    n_model = lax.axis_size("mp")
    devices = n_data * n_model
    owned_rel = relation_table.shape[1]
    translation = lax.all_gather(jnp.sum(relation_table, 0), ("dp", "mp"), axis=0, tiled=True)
    rel_wanted = relation_requests[0]
    owner_base = (
        jnp.arange(n_data, dtype=jnp.int32)[:, None] * n_model
        + jnp.arange(n_model, dtype=jnp.int32)[None, :]
    ) * owned_rel
    rel_global = (rel_wanted + owner_base[:, :, None]).reshape(-1)
    valid_all = edge_valid.astype(jnp.float32)
    negatives_total = neg_slot.shape[2] * n_model
    pairs = lax.psum(jnp.sum(valid_all), ("dp", "mp")) * negatives_total
    wanted = requests[0]
    incoming = lax.all_to_all(
        lax.all_to_all(wanted, "dp", split_axis=0, concat_axis=0, tiled=True),
        "mp",
        split_axis=1,
        concat_axis=1,
        tiled=True,
    )
    served = entity_table[incoming]
    fetched = lax.all_to_all(
        lax.all_to_all(served, "dp", split_axis=0, concat_axis=0, tiled=True),
        "mp",
        split_axis=1,
        concat_axis=1,
        tiled=True,
    )
    slot_count = fetched.shape[0] * fetched.shape[1] * fetched.shape[2]
    fetched = fetched.reshape(slot_count, width)
    slot_grad = jnp.zeros((slot_count, width), jnp.float32)
    relation_sum = jnp.zeros((rel_global.shape[0], width), jnp.float32)
    loss_part = jnp.zeros((), jnp.float32)
    for batch_index in range(src_slot.shape[0]):
        valid_row = valid_all[batch_index]
        own_negatives = fetched[neg_slot[batch_index, 0]]
        negative_rows = lax.all_gather(own_negatives, "mp", axis=0, tiled=True)
        rel_rows = rel_global[relation_ids[batch_index]]
        heads = fetched[src_slot[batch_index]] + translation[rel_rows]
        tails = fetched[dst_slot[batch_index]]
        kept, part_sum = score_forward(heads, tails, negative_rows, valid_row)
        loss_part = loss_part + part_sum
        grad_head, grad_tail, along = score_backward(heads, negative_rows, valid_row, kept, pairs)
        pulled = lax.dot_general(
            along,
            heads,
            (((0,), (0,)), ((), ())),
            precision=HIGH,
            preferred_element_type=jnp.float32,
        )
        grad_negative = lax.psum_scatter(
            pulled - jnp.sum(along, 0)[:, None] * negative_rows,
            "mp",
            scatter_dimension=0,
            tiled=True,
        )
        slot_grad = slot_grad.at[src_slot[batch_index]].add(grad_head)
        slot_grad = slot_grad.at[dst_slot[batch_index]].add(grad_tail)
        slot_grad = slot_grad.at[neg_slot[batch_index, 0]].add(grad_negative)
        relation_sum = relation_sum.at[relation_ids[batch_index]].add(grad_head)
    returned = lax.all_to_all(
        lax.all_to_all(
            slot_grad.reshape(served.shape), "dp", split_axis=0, concat_axis=0, tiled=True
        ),
        "mp",
        split_axis=1,
        concat_axis=1,
        tiled=True,
    )
    entity_grad = (
        jnp.zeros(entity_table.shape, jnp.float32)
        .at[incoming.reshape(-1)]
        .add(returned.reshape(-1, width))
    )
    rel_incoming = lax.all_to_all(
        lax.all_to_all(rel_wanted, "dp", split_axis=0, concat_axis=0, tiled=True),
        "mp",
        split_axis=1,
        concat_axis=1,
        tiled=True,
    )
    rel_returned = lax.all_to_all(
        lax.all_to_all(
            relation_sum.reshape(rel_wanted.shape + (width,)),
            "dp",
            split_axis=0,
            concat_axis=0,
            tiled=True,
        ),
        "mp",
        split_axis=1,
        concat_axis=1,
        tiled=True,
    )
    relation_shard = (
        jnp.zeros((owned_rel, width), jnp.float32)
        .at[rel_incoming.reshape(-1)]
        .add(rel_returned.reshape(-1, width))
    )
    layers = relation_table.shape[0]
    relation_grad = jnp.broadcast_to(relation_shard[None], (layers,) + relation_shard.shape)
    entity_count = entity_table.shape[0] * devices
    relation_count = relation_shard.shape[0] * devices
    ent_rows, ent_colsq, ent_rsum, ent_weighted = local_moments(entity_grad, entity_rows)
    rel_rows, rel_colsq, rel_rsum, rel_weighted = jax.vmap(local_moments, in_axes=(None, 0))(
        relation_shard, relation_rows
    )
    totals = lax.psum((loss_part, ent_colsq, ent_rsum, rel_colsq, rel_rsum), ("dp", "mp"))
    loss_total, ent_colsq, ent_rsum, rel_colsq, rel_rsum = totals
    ent_cols = DECAY * entity_cols + (1.0 - DECAY) * ent_colsq / entity_count
    rel_cols = DECAY * relation_cols + (1.0 - DECAY) * rel_colsq / relation_count
    ent_mean = ent_rsum / entity_count
    rel_mean = rel_rsum / relation_count
    ent_update = scaled_update(entity_grad, ent_rows, ent_cols, ent_mean)
    rel_update = jax.vmap(scaled_update, in_axes=(None, 0, 0, 0))(
        relation_shard, rel_rows, rel_cols, rel_mean
    )
    ent_usq, rel_usq = lax.psum(
        (jnp.sum(ent_update * ent_update), jnp.sum(rel_update * rel_update, (1, 2))), ("dp", "mp")
    )
    ent_factor = jnp.maximum(1.0, jnp.sqrt(ent_usq / (entity_count * width)) / CLIP)
    rel_factor = jnp.maximum(1.0, jnp.sqrt(rel_usq / (relation_count * width)) / CLIP)
    entity_weight = entity_table - LEARN * (ent_update / ent_factor)
    relation_weight = relation_table - LEARN * (rel_update / rel_factor[:, None, None])
    loss = jnp.stack([loss_total, pairs])
    return (
        loss,
        entity_weight,
        entity_grad,
        ent_rows,
        ent_cols,
        entity_weight.astype(jnp.bfloat16),
        relation_weight,
        relation_grad,
        rel_rows,
        rel_cols,
        relation_weight.astype(jnp.bfloat16),
    )


F32, BF16 = jnp.float32, jnp.bfloat16
LOG2E = 1.4426950408889634
OUT_OF_REACH = 1e30
AUX = 16
LANES = 128
MESH = pl.DeviceIdType.MESH


def two(x):
    hi = x.astype(BF16)
    return hi, (x - hi.astype(F32)).astype(BF16)


def three(x):
    hi = x.astype(BF16)
    rest = x - hi.astype(F32)
    mid = rest.astype(BF16)
    return hi, mid, (rest - mid.astype(F32)).astype(BF16)


def mm(a, b):
    return lax.dot_general(a, b, (((1,), (0,)), ((), ())), preferred_element_type=F32)


def mm_t(a, b):
    return lax.dot_general(a, b, (((1,), (1,)), ((), ())), preferred_element_type=F32)


def iota(shape, axis):
    return lax.broadcasted_iota(jnp.int32, shape, axis)


def stack_rows(rows, count, width):
    at = iota((count, width), 0)
    out = jnp.zeros((count, width), F32)
    for i, row in enumerate(rows):
        out = jnp.where(at == i, row, out)
    return out


def stack_columns(columns, height):
    at = iota((height, LANES), 1)
    out = jnp.zeros((height, LANES), F32)
    for i, column in enumerate(columns):
        out = jnp.where(at == i, column, out)
    return out


def pack(rows, out, tail):
    devices, cap = out.shape[0], 8
    width = rows.shape[1]
    full, rest = width // LANES, width % LANES
    for k in range(full):
        out[:, k * cap:(k + 1) * cap, :] = rows[:, k * LANES:(k + 1) * LANES].reshape(devices, cap, LANES)
    tail[:, 0:rest] = rows[:, full * LANES:]
    line = jnp.concatenate([tail[pl.ds(s, devices, stride=cap), 0:rest] for s in range(cap)], 1)
    out[:, full * cap:, :] = line.reshape(devices, 1, LANES)


def unpack(block, tail):
    devices, cap = block.shape[0], 8
    full = block.shape[1] // cap
    rest = LANES // cap
    parts = [block[:, k * cap:(k + 1) * cap, :].reshape(devices * cap, LANES) for k in range(full)]
    line = block[:, full * cap:, :].reshape(devices, LANES)
    for s in range(cap):
        tail[pl.ds(s, devices, stride=cap), 0:rest] = line[:, s * rest:(s + 1) * rest]
    return jnp.concatenate(parts + [tail[:, 0:rest]], 1)


class Spread:
    def __init__(self, me, devices, place, src, dst, send_sem, recv_sem):
        self.me, self.devices, self.place = me, devices, place
        self.src, self.dst, self.send_sem, self.recv_sem = src, dst, send_sem, recv_sem

    def copy(self, p, at):
        return pltpu.make_async_remote_copy(
            src_ref=self.src(p),
            dst_ref=self.dst(at),
            send_sem=self.send_sem.at[p],
            recv_sem=self.recv_sem.at[at],
            device_id=self.place(p),
            device_id_type=MESH,
        )

    def each(self, act):
        def step(i, carry):
            act(lax.rem(self.me + i, self.devices))
            return carry

        lax.fori_loop(1, self.devices, step, 0)

    def start(self):
        self.each(lambda p: self.copy(p, self.me).start())

    def arrived(self):
        self.each(lambda p: self.copy(p, p).wait_recv())

    def left(self):
        self.each(lambda p: self.copy(p, self.me).wait_send())


def step_kernel(
    n_mp, cap, negatives, rb,
    ent_ref, rel_ref, req_ref, rel_req_ref, src_ref, dst_ref, rid_ref, val_ref, neg_slot_ref,
    ent_rows_ref, rel_rows_ref, ent_cols_ref, rel_cols_ref,
    ent_back_ref, rel_back_ref, ids_ref, whole_ref, ent_col_ref, rel_col_ref, step_ref, loss_ref,
    ent_s, rel_s, ent_parts, rel_parts, ask_s, asked, out_ent, out_rel, in_ent, in_rel, back_in_ent, back_in_rel,
    packed, tail_s, counts_s, neg_s, oh_s, oh_d, lead_s, gap_s, head_s, along_s, a_s, b1_s, b2_s, table, neg_rows, neg_parts, count_s,
    acc_s, gn_s, from_mate, from_across, part_mp, part_dp, loss_s, pull_s, weight_s, near_s, bound_s,
    load_sem, ask_send, ask_recv, ent_send, ent_recv, rel_send, rel_recv, mp_send, mp_recv,
    forward_send, forward_recv, count_send, count_recv,
    back_ent_send, back_ent_recv, back_rel_send, back_rel_recv, mate_send, mate_recv,
    sum_mp_send, sum_mp_recv, sum_dp_send, sum_dp_recv,
):
    width, owned = ent_s.shape
    layers, _, owned_rel = rel_s.shape
    devices = out_ent.shape[0]
    n_dp = devices // n_mp
    slots = devices * cap
    batches, edges = src_ref.shape
    main = width // LANES * LANES
    rest = width - main
    dp, mp = lax.axis_index("dp"), lax.axis_index("mp")
    me = dp * n_mp + mp
    mate, across = mp + 1 - 2 * lax.rem(mp, 2), lax.rem(mp + 2, n_mp)
    beyond = mate + across - mp

    def place(p):
        return lax.div(p, n_mp), lax.rem(p, n_mp)

    def by_columns(size, act):
        blocks = edges // size

        def step(t, carry):
            act(lax.div(t, blocks), pl.ds(pl.multiple_of(lax.rem(t, blocks) * size, size), size))
            return carry

        lax.fori_loop(0, batches * blocks, step, 0)

    block_of = lambda size: size if edges % size == 0 else edges
    narrow, broad = block_of(512), block_of(1024)

    barrier = pltpu.get_barrier_semaphore()

    def tell(i, carry):
        pl.semaphore_signal(
            barrier, inc=1, device_id=place(lax.rem(me + i, devices)), device_id_type=MESH
        )
        return carry

    lax.fori_loop(1, devices, tell, 0)
    load_ent = pltpu.make_async_copy(ent_ref, ent_s, load_sem.at[0])
    load_rel = pltpu.make_async_copy(rel_ref, rel_s, load_sem.at[1])
    load_ent.start()
    load_rel.start()
    valid = jnp.sum(jnp.sum(val_ref[...], 0, keepdims=True), 1, keepdims=True)
    lane = iota(ask_s.shape, 2)
    ask_s[...] = jnp.where(lane == 2 * cap, valid[None], 0)
    ask_s[:, :, 0:cap] = req_ref[0]
    ask_s[:, :, cap:2 * cap] = rel_req_ref[0]
    asked[me] = ask_s[dp, pl.ds(mp, 1)]
    ask = Spread(
        me, devices, place, lambda p: ask_s.at[place(p)[0], pl.ds(place(p)[1], 1)], lambda p: asked.at[p], ask_send, ask_recv
    )
    pl.semaphore_wait(barrier, devices - 1)

    ask.start()
    load_ent.wait()
    load_rel.wait()
    rows_at = 80 if width % 80 == 0 else width

    def split(t, carry):
        span = pl.ds(pl.multiple_of(t * rows_at, rows_at), rows_at)
        for i, part in enumerate(two(ent_s[span, :])):
            ent_parts[i, span, :] = part
        for i, part in enumerate(two(sum(rel_s[i, span, :] for i in range(layers)))):
            rel_parts[i, span, 0:owned_rel] = part
        return carry

    lax.fori_loop(0, width // rows_at, split, 0)
    if rel_parts.shape[2] > owned_rel:
        rel_parts[:, :, owned_rel:] = jnp.zeros((2, width, rel_parts.shape[2] - owned_rel), BF16)
    ask.arrived()
    wide = jnp.broadcast_to(asked[...], (devices, cap, LANES)).reshape(slots, LANES)
    at, lane = lax.rem(iota(wide.shape, 0), cap), iota(wide.shape, 1)
    ent_id = jnp.sum(jnp.where(lane == at, wide, 0), 1, keepdims=True)
    rel_id = jnp.sum(jnp.where(lane == at + cap, wide, 0), 1, keepdims=True)

    pick = jnp.where(iota((slots, owned), 1) == ent_id, 1.0, 0.0).astype(BF16)
    rows = mm_t(pick, ent_parts[0]) + mm_t(pick, ent_parts[1])
    pick = jnp.where(iota((slots, rel_parts.shape[2]), 1) == rel_id, 1.0, 0.0).astype(BF16)
    rel_rows = mm_t(pick, rel_parts[0]) + mm_t(pick, rel_parts[1])

    def block(ref):
        return lambda p: ref.at[p]

    pack(rows, out_ent, tail_s.at[0])
    give_ent = Spread(me, devices, place, block(out_ent), block(in_ent), ent_send, ent_recv)
    give_ent.start()
    pack(rel_rows, out_rel, tail_s.at[1])
    give_rel = Spread(me, devices, place, block(out_rel), block(in_rel), rel_send, rel_recv)
    give_rel.start()
    in_ent[me] = out_ent[me]
    in_rel[me] = out_rel[me]
    ids_ref[...] = jnp.where(iota(ids_ref.shape, 1) == 0, ent_id, jnp.where(iota(ids_ref.shape, 1) == 1, rel_id, 0))
    valid_all = jnp.sum(jnp.where(iota(asked.shape, 2) == 2 * cap, asked[...], 0), 0)
    pairs = jnp.sum(valid_all, 1, keepdims=True).astype(F32) * negatives
    slot = iota((slots, narrow), 0)

    def mark(m, cols):
        row = pl.ds(m, 1)
        oh_s[m, 0:slots, cols] = jnp.where(slot == src_ref[row, cols], 1.0, 0.0).astype(BF16)
        oh_s[m, slots:, cols] = jnp.where(slot == rid_ref[row, cols], 1.0, 0.0).astype(BF16)
        oh_d[m, :, cols] = jnp.where(slot == dst_ref[row, cols], 1.0, 0.0).astype(BF16)

    by_columns(narrow, mark)
    hits = [
        jnp.sum(jnp.where(iota((slots, neg_slot_ref.shape[2]), 0) == neg_slot_ref[m], 1.0, 0.0), 1, keepdims=True)
        for m in range(batches)
    ]
    counts_s[mp] = stack_columns(hits, slots).T[0:8]
    count_copies = []
    for i in range(1, n_mp):
        count_copies.append(pltpu.make_async_remote_copy(
            src_ref=counts_s.at[mp], dst_ref=counts_s.at[mp], send_sem=count_send.at[i], recv_sem=count_recv.at[i],
            device_id=(dp, lax.rem(mp + i, n_mp)), device_id_type=MESH,
        ))
        count_copies[-1].start()
    ask.left()

    def forward(p):
        return pltpu.make_async_remote_copy(
            src_ref=in_ent.at[p], dst_ref=packed.at[0, p], send_sem=forward_send.at[p], recv_sem=forward_recv.at[p],
            device_id=(dp, across), device_id_type=MESH,
        )

    forward(me).start()

    def pass_on(p):
        give_ent.copy(p, p).wait_recv()
        forward(p).start()

    give_ent.each(pass_on)

    def hand(i, src, dst):
        return pltpu.make_async_remote_copy(
            src_ref=src, dst_ref=packed.at[dst], send_sem=mp_send.at[i], recv_sem=mp_recv.at[i],
            device_id=(dp, mate), device_id_type=MESH,
        )

    to_mate, onward = hand(0, in_ent, 1), hand(1, packed.at[0], 2)
    to_mate.start()
    own_t = unpack(in_ent, tail_s.at[0]).T
    neg_s[3] = own_t
    for i, part in enumerate(two(own_t)):
        table[i, :, 0:slots] = part
    def start_of_head(m, cols):
        lead = mm(table[0, :, 0:slots], oh_s[m, 0:slots, cols]) + mm(table[1, :, 0:slots], oh_s[m, 0:slots, cols])
        lead_s[m, :, cols] = lead
        gap_s[m, :, cols] = lead - mm(table[0, :, 0:slots], oh_d[m, :, cols]) - mm(table[1, :, 0:slots], oh_d[m, :, cols])

    by_columns(narrow, start_of_head)

    give_rel.arrived()
    rel_got = unpack(in_rel, tail_s.at[1]).T
    for i, part in enumerate(two(rel_got)):
        table[i, :, slots:] = part
    def whole_head(m, cols):
        moved = mm(table[0, :, slots:], oh_s[m, slots:, cols]) + mm(table[1, :, slots:], oh_s[m, slots:, cols])
        head = lead_s[m, :, cols] + moved
        diff = gap_s[m, :, cols] + moved
        near2 = jnp.sum(diff * diff, 0, keepdims=True) + EPS_DIST
        inv_near = lax.rsqrt(near2)
        near_s[m, :, cols] = inv_near
        bound_s[m, :, cols] = jnp.where(
            val_ref[pl.ds(m, 1), cols] > 0, (MARGIN + near2 * inv_near) * LOG2E, -OUT_OF_REACH
        )
        norm = three((jnp.sum(head * head, 0, keepdims=True) + EPS_DIST) * (LOG2E * LOG2E))
        ones = jnp.ones_like(near2)
        head_s[m, 0:width, cols] = head.astype(BF16)
        extra = stack_rows([ones] * 3 + [part.astype(F32) for part in norm], AUX, near2.shape[1])
        head_s[m, width:, cols] = extra.astype(BF16)

    by_columns(broad, whole_head)
    order = (across, beyond, mate, mp)

    def ready(g):
        if g == 0:
            def came(p, carry):
                forward(p).wait_recv()
                return carry

            lax.fori_loop(0, devices, came, 0)
            onward.start()
            for i in range(1, n_mp):
                from_mp = lax.rem(mp + n_mp - i, n_mp)
                pltpu.make_async_remote_copy(
                    src_ref=counts_s.at[mp], dst_ref=counts_s.at[from_mp], send_sem=count_send.at[i],
                    recv_sem=count_recv.at[i], device_id=(dp, from_mp), device_id_type=MESH,
                ).wait_recv()
        elif g == 1:
            onward.wait_recv()
        elif g == 2:
            to_mate.wait_recv()
        if g < 3:
            neg_s[g] = unpack(packed.at[(0, 2, 1)[g]], tail_s.at[0]).T
        n = neg_s[g]
        norm = three(jnp.sum(n * n, 0, keepdims=True) * (LOG2E * LOG2E))
        ones = jnp.ones((1, slots), F32)
        extra = stack_rows([part.astype(F32) for part in norm] + [ones] * 3, AUX, slots)
        neg_rows[g] = jnp.concatenate([n * (-2.0 * LOG2E * LOG2E), extra], 0).T.astype(BF16)
        for i, part in enumerate(two(n)):
            neg_parts[i, :, g * slots:(g + 1) * slots] = part
        blank = jnp.zeros((LANES - 8, slots), F32)
        count_s[g] = jnp.concatenate([counts_s[order[g]], blank], 0).T

    loss_s[...] = jnp.zeros_like(loss_s)
    weight = [jnp.zeros((8, edges), F32) for _ in range(batches)]
    pulls = [jnp.zeros((8, edges), F32) for _ in range(batches)]

    steps = [(g, m) for g in range(n_mp) for m in range(batches)]
    pieces = slots // rb

    def distances(i, b):
        g, m = steps[i]
        part = slice(b * edges // pieces, (b + 1) * edges // pieces)
        lead_s[i % 2, 0:slots, part] = mm(neg_rows[g], head_s[m, :, part])

    def pair_terms(i, b):
        g, m = steps[i]
        span = slice(b * rb, (b + 1) * rb)
        count = count_s[g, span, m:m + 1]
        square = jnp.maximum(lead_s[i % 2, span, :], 1e-20)
        inv_far = lax.rsqrt(square)
        t = square * inv_far - bound_s[m]
        sig = pl.reciprocal(1.0 + jnp.exp2(t), approx=True)
        rest_sig = 1.0 - sig
        low, high = jnp.minimum(sig, rest_sig), jnp.maximum(sig, rest_sig)
        w = count * sig
        pulls[m] = pulls[m] + jnp.sum(w.reshape(rb // 8, 8, edges), 0)
        w = w * inv_far
        weight[m] = weight[m] + jnp.sum(w.reshape(rb // 8, 8, edges), 0)
        along_s[i % 2, span, :] = w.astype(BF16)
        q = jnp.zeros((rb, LANES), F32)
        over = jnp.zeros((rb, LANES), F32)
        for k in range(edges // LANES):
            part = slice(k * LANES, (k + 1) * LANES)
            q = q * high[:, part] + low[:, part]
            over = over + jnp.minimum(t[:, part], 0.0)
        term = count * (-jnp.log(1.0 - q) - over * (1.0 / LOG2E))
        loss_s[...] += jnp.sum(term.reshape(rb // 8, 8, LANES), 0)

    def by_slot(i, half):
        g, m = steps[i]
        rows = slice(half * slots, (half + 1) * slots)
        part = mm_t(oh_s[m, rows, :], along_s[i % 2])
        a_s[g, rows, :] = part if m == 0 else a_s[g, rows, :] + part

    def grads_of(g):
        total = a_s[g] * LOG2E
        hi, lo = two(total)
        whole = jnp.sum(total[0:slots], 0, keepdims=True)
        cols = slice(g * slots, (g + 1) * slots)
        slot_part = mm_t(hi, neg_parts[0, :, cols]) + mm_t(hi, neg_parts[1, :, cols]) + mm_t(lo, neg_parts[0, :, cols])
        acc_s[...] = slot_part if g == 0 else acc_s[...] + slot_part
        return mm(table[0], hi) + mm(table[1], hi) + mm(table[0], lo) - whole * neg_s[g]

    def swap(i, src, dst, to):
        return pltpu.make_async_remote_copy(
            src_ref=src, dst_ref=dst, send_sem=mate_send.at[i], recv_sem=mate_recv.at[i],
            device_id=(dp, to), device_id_type=MESH,
        )

    through = swap(0, gn_s.at[0], from_mate.at[0], mate)
    over_x = swap(1, gn_s.at[1], from_across, across)
    direct = swap(2, gn_s.at[2], from_mate.at[1], mate)
    def group_done(g):
        grad = grads_of(g)
        if g == 0:
            gn_s[1] = grad
        elif g == 1:
            gn_s[0] = grad
            through.start()
        elif g == 2:
            gn_s[2] = grad
            direct.start()
        else:
            gn_s[3] = grad

    ready(0)
    for b in range(pieces):
        distances(0, b)
    for i in range(len(steps)):
        if i + 1 < len(steps) and steps[i + 1][1] == 0:
            ready(steps[i + 1][0])
        for b in range(pieces):
            if i + 1 < len(steps):
                distances(i + 1, b)
            pair_terms(i, b)
        by_slot(i, 0)
        by_slot(i, 1)
        if steps[i][1] == batches - 1:
            group_done(steps[i][0])
        if i == 2 * batches:
            through.wait_recv()
            gn_s[1] = gn_s[1] + from_mate[0]
            over_x.start()

    broad_slot = iota((slots, broad), 0)
    for m in range(batches):
        pull_s[m] = pulls[m]
        weight_s[m] = weight[m]
    b1_s[...] = jnp.zeros_like(b1_s)
    b2_s[...] = jnp.zeros_like(b2_s)

    def edge_weights(m, cols):
        row = pl.ds(m, 1)
        pull = jnp.sum(pull_s[m, :, cols], 0, keepdims=True) * near_s[m, :, cols]
        excess = pull - jnp.sum(weight_s[m, :, cols], 0, keepdims=True) * LOG2E
        hit = broad_slot == dst_ref[row, cols]
        b1_s[...] += sum(
            mm_t(oh_s[m, :, cols], jnp.where(hit, piece.astype(F32), 0.0).astype(BF16)) for piece in two(pull)
        )
        hit = broad_slot == rid_ref[row, cols]
        b2_s[...] += sum(
            mm_t(oh_s[m, 0:slots, cols], jnp.where(hit, piece.astype(F32), 0.0).astype(BF16)) for piece in two(excess)
        )

    by_columns(broad, edge_weights)
    sd, rd, sr = b1_s[0:slots, :], b1_s[slots:, :], b2_s[...]
    eye = iota((slots, slots), 0) == iota((slots, slots), 1)
    ss = jnp.where(eye, jnp.sum(sr, 1, keepdims=True) + jnp.sum(sd, 0, keepdims=True), 0.0) - sd - sd.T
    rr = jnp.where(eye, jnp.sum(sr, 0, keepdims=True), 0.0)
    cross = sr - rd.T

    def grads(lo, hi, left, right):
        kept = two(jnp.concatenate([left, right], 1))
        return acc_s[lo:hi, :] + mm_t(kept[0], table[0]) + mm_t(kept[0], table[1]) + mm_t(kept[1], table[0])

    grad_rel = grads(slots, 2 * slots, cross.T, rr)
    give_ent.left()
    give_rel.left()
    pack(grad_rel, out_rel, tail_s.at[1])
    back_rel = Spread(me, devices, place, block(out_rel), block(back_in_rel), back_rel_send, back_rel_recv)
    back_ent = Spread(me, devices, place, block(out_ent), block(back_in_ent), back_ent_send, back_ent_recv)
    back_rel.start()
    grad_ent = grads(0, slots, ss, cross)
    direct.wait_recv()
    over_x.wait_recv()
    grad_ent = grad_ent + (gn_s[3] + from_mate[1] + from_across[...]).T
    pack(grad_ent, out_ent, tail_s.at[0])
    back_ent.start()
    back_in_rel[me] = out_rel[me]
    back_in_ent[me] = out_ent[me]

    def same_rows(column, rows, height):
        row = jnp.broadcast_to(column.astype(F32), (slots, LANES)).T[0:1]
        same = jnp.where(column.astype(F32) == row, 1.0, 0.0)
        share_of = 1.0 / jnp.sum(same, 1, keepdims=True)
        hit = iota((slots, height), 1) == column
        old = [jnp.sum(jnp.where(hit, r, 0.0), 1, keepdims=True) for r in rows]
        kept = [jnp.sum(DECAY * r + (1.0 - DECAY) * EPS_SQ, 1, keepdims=True) for r in rows]
        return same.astype(BF16), share_of, old, kept

    ent_same = same_rows(ent_id, [ent_rows_ref[...]], owned)
    rel_same = same_rows(rel_id, [rel_rows_ref[layer:layer + 1, :] for layer in range(layers)], owned_rel)
    scale = 1.0 / pairs

    def row_sums(back, same, share_of, old, kept):
        grad = sum(mm(same, part) for part in two(back))
        square = grad * grad
        whole = jnp.sum(square, 1, keepdims=True)
        moment = (1.0 - DECAY) / width * whole
        out = [jnp.sum(square * share_of, 0, keepdims=True)]
        sums = []
        for o, k in zip(old, kept):
            new = DECAY * o + (1.0 - DECAY) * EPS_SQ + moment
            out.append(jnp.sum(square * (share_of / new), 0, keepdims=True))
            sums.append(k + jnp.sum(moment * share_of, 0, keepdims=True))
        return whole, out, sums

    back_rel.arrived()
    rel_back = unpack(back_in_rel, tail_s.at[1]) * scale
    rel_whole, more_rows, more_sums = row_sums(rel_back, *rel_same)
    back_ent.arrived()
    ent_back = unpack(back_in_ent, tail_s.at[0]) * scale
    ent_whole, rows, sums = row_sums(ent_back, *ent_same)
    rows = rows + more_rows
    scalars = [jnp.sum(jnp.sum(loss_s[...], 0, keepdims=True), 1, keepdims=True)] + sums + more_sums
    full = main // LANES
    tails = [row[:, main:] for row in rows] + scalars
    tails.append(jnp.zeros((1, LANES - rest * len(rows) - len(scalars)), F32))
    lines = [row[:, i * LANES:(i + 1) * LANES] for row in rows for i in range(full)]
    part_mp[mp] = stack_rows(lines + [jnp.concatenate(tails, 1)], 16, LANES)

    def share(axis, size, at, buffer, send, recv, meanwhile):
        copies = []
        for i in range(1, size):
            copies.append(pltpu.make_async_remote_copy(
                src_ref=buffer.at[at], dst_ref=buffer.at[at], send_sem=send.at[i], recv_sem=recv.at[i],
                device_id={axis: lax.rem(at + i, size)}, device_id_type=MESH,
            ))
            copies[-1].start()
        meanwhile()
        for i in range(1, size):
            came = lax.rem(at + size - i, size)
            pltpu.make_async_remote_copy(
                src_ref=buffer.at[came], dst_ref=buffer.at[came], send_sem=send.at[i], recv_sem=recv.at[i],
                device_id={axis: came}, device_id_type=MESH,
            ).wait_recv()
        return copies

    def write_out():
        ent_back_ref[...] = ent_back.T
        rel_back_ref[...] = rel_back.T
        lane = iota(whole_ref.shape, 1)
        whole_ref[...] = jnp.where(lane == 0, ent_whole, jnp.where(lane == 1, rel_whole, 0.0))

    def settle():
        for copy in [to_mate, onward, through, over_x, direct] + count_copies:
            copy.wait_send()

        def gone(p, carry):
            forward(p).wait_send()
            return carry

        lax.fori_loop(0, devices, gone, 0)
        back_rel.left()
        back_ent.left()

    copies = share("mp", n_mp, mp, part_mp, sum_mp_send, sum_mp_recv, write_out)
    part_dp[dp] = jnp.sum(part_mp[...], 0)
    copies += share("dp", n_dp, dp, part_dp, sum_dp_send, sum_dp_recv, settle)
    total = jnp.sum(part_dp[...], 0)
    last = total[len(lines):len(lines) + 1, :]
    summed = [
        jnp.concatenate(
            [total[i * full + k:i * full + k + 1, :] for k in range(full)] + [last[:, i * rest:(i + 1) * rest]], 1
        )
        for i in range(len(rows))
    ]
    single = [last[:, rest * len(rows) + i:rest * len(rows) + i + 1] for i in range(len(scalars))]

    def finish(cols, col_sum, weighted, moment_sum, height):
        new = DECAY * cols + (1.0 - DECAY) * (col_sum / height + EPS_SQ)
        mean = moment_sum / height
        square = jnp.sum(weighted / new, 1, keepdims=True) * mean
        factor = jnp.maximum(1.0, jnp.sqrt(square / (height * width)) / CLIP)
        return new, LEARN * jnp.sqrt(mean) * lax.rsqrt(new) / factor

    new, step = finish(
        ent_cols_ref[...], summed[0], summed[1], single[1], owned * devices
    )
    ent_col_ref[...] = new
    moves = [step]
    for layer in range(layers):
        new, step = finish(
            rel_cols_ref[layer:layer + 1, :], summed[2], summed[3 + layer], single[2 + layer], owned_rel * devices,
        )
        rel_col_ref[layer:layer + 1, :] = new
        moves.append(step)
    step_ref[...] = stack_rows(moves, LANES, width).T
    lane = iota(loss_ref.shape, 1)
    loss_ref[...] = jnp.where(lane == 0, single[0], jnp.where(lane == 1, pairs, 0.0))
    for copy in copies:
        copy.wait_send()


def update_kernel(
    ent_ref, rel_ref, ent_back_ref, rel_back_ref, ids_ref, whole_ref, ent_rows_ref, rel_rows_ref, step_ref,
    ent_cols_ref, rel_cols_ref, loss_ref,
    ent_w_ref, ent_g_ref, ent_c_ref, rel_w_ref, rel_g_ref, rel_c_ref,
    ent_new_ref, rel_new_ref, ent_col_ref, rel_col_ref, loss_out_ref,
    ent_pick, rel_pick,
):
    layers = rel_ref.shape[0]
    width = ent_cols_ref.shape[1]

    @pl.when(pl.program_id(0) == 0)
    def _():
        def moments(pick, which, old):
            hit = iota(pick.shape, 1) == ids_ref[:, which:which + 1]
            pick[...] = jnp.where(hit, 1.0, 0.0).astype(BF16)
            whole = jnp.max(jnp.where(hit, whole_ref[:, which:which + 1], 0.0), 0, keepdims=True)
            return DECAY * old + (1.0 - DECAY) * (whole / width + EPS_SQ)

        ent_new_ref[...] = moments(ent_pick, 0, ent_rows_ref[...])
        rel_new_ref[...] = moments(rel_pick, 1, rel_rows_ref[...])
        ent_col_ref[...] = ent_cols_ref[...]
        rel_col_ref[...] = rel_cols_ref[...]
        for i in range(2):
            loss_out_ref[i] = loss_ref[0, i]

    grad = sum(mm(part, ent_pick[...]) for part in two(ent_back_ref[...]))
    ent_g_ref[...] = grad
    new = ent_ref[...] - grad * lax.rsqrt(ent_new_ref[...]) * step_ref[:, 0:1]
    ent_w_ref[...] = new
    ent_c_ref[...] = new.astype(BF16)
    grad = sum(mm(part, rel_pick[...]) for part in two(rel_back_ref[...]))
    for layer in range(layers):
        rel_g_ref[layer] = grad
        new = rel_ref[layer] - grad * lax.rsqrt(rel_new_ref[layer:layer + 1, :]) * step_ref[:, layer + 1:layer + 2]
        rel_w_ref[layer] = new
        rel_c_ref[layer] = new.astype(BF16)


def fused(
    entity_table, entity_rows, entity_cols, relation_table, relation_rows, relation_cols,
    requests, relation_requests, src_slot, dst_slot, relation_ids, edge_valid, neg_slot,
):
    n_mp, n_dp = lax.axis_size("mp"), lax.axis_size("dp")
    devices = n_dp * n_mp
    cap = requests.shape[3]
    slots = devices * cap
    negatives = neg_slot.shape[2] * n_mp
    ent_t = entity_table.T
    rel_t = jnp.swapaxes(relation_table, 1, 2)
    width, owned = ent_t.shape
    layers, _, owned_rel = rel_t.shape
    batches, edges = src_slot.shape
    lines = cap * width // LANES
    padded_rel = -(-owned_rel // LANES) * LANES
    V, sem = pltpu.VMEM, pltpu.SemaphoreType.DMA
    vmem = pl.BlockSpec(memory_space=pltpu.VMEM)
    hbm = pl.BlockSpec(memory_space=pl.ANY)
    shape = jax.ShapeDtypeStruct
    args = (
        ent_t, rel_t, requests, relation_requests, src_slot, dst_slot, relation_ids, edge_valid, neg_slot,
        entity_rows[None], relation_rows, entity_cols[None], relation_cols,
    )
    outs = [
        shape((width, slots), F32), shape((width, slots), F32), shape((slots, LANES), jnp.int32),
        shape((slots, LANES), F32), shape((1, width), F32), shape((layers, width), F32),
        shape((width, LANES), F32), shape((8, LANES), F32),
    ]
    many = sem((devices,))
    ent_back, rel_back, ids, whole, ent_col, rel_col, steps, loss = pl.pallas_call(
        functools.partial(step_kernel, n_mp, cap, negatives, 32),
        out_shape=outs,
        in_specs=[hbm, hbm] + [vmem] * (len(args) - 2),
        out_specs=[vmem] * len(outs),
        scratch_shapes=[
            V((width, owned), F32), V((layers, width, owned_rel), F32),
            V((2, width, owned), BF16), V((2, width, padded_rel), BF16),
            V((n_dp, n_mp, LANES), jnp.int32), V((devices, 1, LANES), jnp.int32),
            V((devices, lines, LANES), F32), V((devices, lines, LANES), F32),
            V((devices, lines, LANES), F32), V((devices, lines, LANES), F32),
            V((devices, lines, LANES), F32), V((devices, lines, LANES), F32),
            V((3, devices, lines, LANES), F32), V((2, slots, LANES), F32), V((n_mp, 8, slots), F32), V((n_mp, width, slots), F32),
            V((batches, 2 * slots, edges), BF16), V((batches, slots, edges), BF16),
            V((batches, width, edges), F32), V((batches, width, edges), F32), V((batches, width + AUX, edges), BF16),
            V((2, slots, edges), BF16),
            V((n_mp, 2 * slots, slots), F32), V((2 * slots, slots), F32), V((slots, slots), F32),
            V((2, width, 2 * slots), BF16), V((n_mp, slots, width + AUX), BF16), V((2, width, n_mp * slots), BF16),
            V((n_mp, slots, LANES), F32),
            V((2 * slots, width), F32), V((4, width, slots), F32), V((2, width, slots), F32), V((width, slots), F32),
            V((n_mp, 16, LANES), F32), V((n_dp, 16, LANES), F32), V((8, LANES), F32),
            V((batches, 8, edges), F32), V((batches, 8, edges), F32),
            V((batches, 1, edges), F32), V((batches, 1, edges), F32),
            sem((2,)), many, many, many, many, many, many, sem((2,)), sem((2,)),
            many, many, sem((n_mp,)), sem((n_mp,)),
            many, many, many, many, sem((3,)), sem((3,)),
            sem((n_mp,)), sem((n_mp,)), sem((n_dp,)), sem((n_dp,)),
        ],
        compiler_params=pltpu.CompilerParams(
            collective_id=1, has_side_effects=True, vmem_limit_bytes=60 << 20
        ),
        name="step",
    )(*args)
    rows = 80 if width % 80 == 0 else width
    ent_block = pl.BlockSpec((rows, owned), lambda i: (i, 0))
    rel_block = pl.BlockSpec((layers, rows, owned_rel), lambda i: (0, i, 0))
    slot_block = pl.BlockSpec((rows, slots), lambda i: (i, 0))
    fixed = lambda a: pl.BlockSpec(a.shape, lambda i, n=a.ndim: (0,) * n)
    smem = pl.BlockSpec(memory_space=pltpu.SMEM)
    ent_rows, rel_rows = entity_rows[None], relation_rows
    small = (ent_rows, rel_rows, ent_col, rel_col)
    ent_w, ent_g, ent_c, rel_w, rel_g, rel_c, ent_new, rel_new, ent_col, rel_col, loss = pl.pallas_call(
        update_kernel,
        grid=(width // rows,),
        out_shape=[
            shape(ent_t.shape, F32), shape(ent_t.shape, F32), shape(ent_t.shape, BF16),
            shape(rel_t.shape, F32), shape(rel_t.shape, F32), shape(rel_t.shape, BF16),
        ] + [shape(a.shape, F32) for a in small] + [shape((2,), F32)],
        in_specs=[
            ent_block, rel_block, slot_block, slot_block, fixed(ids), fixed(whole), fixed(ent_rows), fixed(rel_rows),
            pl.BlockSpec((rows, LANES), lambda i: (i, 0)), fixed(ent_col), fixed(rel_col), smem,
        ],
        out_specs=[ent_block] * 3 + [rel_block] * 3 + [fixed(a) for a in small] + [smem],
        scratch_shapes=[V((slots, owned), BF16), V((slots, owned_rel), BF16)],
        compiler_params=pltpu.CompilerParams(vmem_limit_bytes=60 << 20),
        name="update",
    )(ent_t, rel_t, ent_back, rel_back, ids, whole, ent_rows, rel_rows, steps, ent_col, rel_col, loss)
    back = lambda x: jnp.swapaxes(x, -1, -2)
    return (
        loss, back(ent_w), back(ent_g), ent_new[0], ent_col[0], back(ent_c),
        back(rel_w), back(rel_g), rel_new, rel_col, back(rel_c),
    )


def solution(mesh):
    in_specs = (
        P(("dp", "mp"), None),
        P(("dp", "mp")),
        P(),
        P(None, ("dp", "mp"), None),
        P(None, ("dp", "mp")),
        P(),
        P(("dp", "mp"), None, None, None),
        P(("dp", "mp"), None, None, None),
        P(None, ("dp", "mp")),
        P(None, ("dp", "mp")),
        P(None, ("dp", "mp")),
        P(None, ("dp", "mp")),
        P(None, "dp", "mp"),
    )
    out_specs = (
        P(),
        P(("dp", "mp"), None),
        P(("dp", "mp"), None),
        P(("dp", "mp")),
        P(),
        P(("dp", "mp"), None),
        P(None, ("dp", "mp"), None),
        P(None, ("dp", "mp"), None),
        P(None, ("dp", "mp")),
        P(),
        P(None, ("dp", "mp"), None),
    )

    def step(*args):
        owners_dp, owners_mp, cap = args[6].shape[1:]
        fits = args[0].shape[0] <= args[8].shape[1] and args[8].shape[1] % 128 == 0
        small = fits and owners_mp == 4 and cap == 8 and owners_dp * owners_mp * cap <= 512
        return (fused if small else shards)(*args)

    return jax.shard_map(step, mesh=mesh, in_specs=in_specs, out_specs=out_specs, check_vma=False)
```

profile of v0, /device:TPU:0, one launch (start us, length us, event | category | flops | bytes accessed | tf_op | source)
XLA Modules:
  0.0 110.5 jit_solution(10280606185653280044)
XLA Ops:
  0.6 99.0 %step.1 = (f32[400,256]{1,0:T(8,128)}, f32[400,256]{1,0:T(8,128)}, s32[256,128]{1,0:T(8,128)}, f32[256,128]{1,0:T(8,128)}, f32[1,400]{1,0:T(1,128)}, /*index=5*/...) custom-call(f32[400,2048]{1,0:T(8,128)} %bitcast.12, f32[2,400,784]{2,1,0:T(8,128)} %bitcast.14, ...), custom_call_target="tpu_custom_call" | custom-call | tf_op jit(solution)/shard_map/step/pallas_call | solution.py:854
  99.6 10.7 %update.1 = (f32[400,2048]{1,0:T(8,128)}, f32[400,2048]{1,0:T(8,128)}, bf16[400,2048]{1,0:T(8,128)(2,1)}, f32[2,400,784]{2,1,0:T(8,128)}, f32[2,400,784]{2,1,0:T...) custom-call(f32[400,2048]{1,0:T(8,128)} %bitcast.13, ...), custom_call_target="tpu_custom_call" | custom-call | tf_op jit(solution)/shard_map/update/pallas_call | solution.py:895
where the time goes:
time: 111 us
  Pallas kernels  110 us (99%)
    pallas_call x1, Pallas kernels, fused(): pl.pallas_call(functools.partial(step_kernel, n_mp, cap, negatives, 32),...  99 us
    pallas_call x1, Pallas kernels, fused(): pl.pallas_call(update_kernel, grid=(width // rows,), out_shape=[shape(ent...  10.7 us

commit v1 on v0

--- a/solution.py
+++ b/solution.py
@@ -318,7 +318,15 @@
 
 def step_kernel(
     n_mp, cap, negatives, rb,
-    ent_ref, rel_ref, req_ref, rel_req_ref, src_ref, dst_ref, rid_ref, val_ref, neg_slot_ref,
+    ent_ref, rel_ref, *refs,
+):
+    inputs, kept = refs[:11], refs[-11:]
+    step_body(n_mp, cap, negatives, rb, ent_ref, rel_ref, inputs, *kept, *refs[11:-11])
+
+
+def step_body(
+    n_mp, cap, negatives, rb, ent_ref, rel_ref, inputs,
+    req_ref, rel_req_ref, src_ref, dst_ref, rid_ref, val_ref, neg_slot_ref,
     ent_rows_ref, rel_rows_ref, ent_cols_ref, rel_cols_ref,
     ent_back_ref, rel_back_ref, ids_ref, whole_ref, ent_col_ref, rel_col_ref, step_ref, loss_ref,
     ent_s, rel_s, ent_parts, rel_parts, ask_s, asked, out_ent, out_rel, in_ent, in_rel, back_in_ent, back_in_rel,
@@ -355,7 +363,7 @@
         lax.fori_loop(0, batches * blocks, step, 0)
 
     block_of = lambda size: size if edges % size == 0 else edges
-    narrow, broad = block_of(512), block_of(1024)
+    narrow, broad = block_of(512), block_of(2048)
 
     barrier = pltpu.get_barrier_semaphore()
 
@@ -368,8 +376,17 @@
     lax.fori_loop(1, devices, tell, 0)
     load_ent = pltpu.make_async_copy(ent_ref, ent_s, load_sem.at[0])
     load_rel = pltpu.make_async_copy(rel_ref, rel_s, load_sem.at[1])
+    kept = (
+        req_ref, rel_req_ref, src_ref, dst_ref, rid_ref, val_ref, neg_slot_ref,
+        ent_rows_ref, rel_rows_ref, ent_cols_ref, rel_cols_ref,
+    )
+    small = [pltpu.make_async_copy(a, b, load_sem.at[2 + i]) for i, (a, b) in enumerate(zip(inputs, kept))]
+    for copy in small:
+        copy.start()
     load_ent.start()
     load_rel.start()
+    for copy in small:
+        copy.wait()
     valid = jnp.sum(jnp.sum(val_ref[...], 0, keepdims=True), 1, keepdims=True)
     lane = iota(ask_s.shape, 2)
     ask_s[...] = jnp.where(lane == 2 * cap, valid[None], 0)
@@ -784,41 +801,88 @@
 
 
 def update_kernel(
+    rows,
     ent_ref, rel_ref, ent_back_ref, rel_back_ref, ids_ref, whole_ref, ent_rows_ref, rel_rows_ref, step_ref,
     ent_cols_ref, rel_cols_ref, loss_ref,
     ent_w_ref, ent_g_ref, ent_c_ref, rel_w_ref, rel_g_ref, rel_c_ref,
     ent_new_ref, rel_new_ref, ent_col_ref, rel_col_ref, loss_out_ref,
-    ent_pick, rel_pick,
+    ent_pick, rel_pick, ent_s, rel_s, ent_w, ent_g, ent_c, rel_w, rel_g, rel_c, load_sem, store_sem, grad_sem,
 ):
-    layers = rel_ref.shape[0]
-    width = ent_cols_ref.shape[1]
-
-    @pl.when(pl.program_id(0) == 0)
-    def _():
-        def moments(pick, which, old):
-            hit = iota(pick.shape, 1) == ids_ref[:, which:which + 1]
-            pick[...] = jnp.where(hit, 1.0, 0.0).astype(BF16)
-            whole = jnp.max(jnp.where(hit, whole_ref[:, which:which + 1], 0.0), 0, keepdims=True)
-            return DECAY * old + (1.0 - DECAY) * (whole / width + EPS_SQ)
-
-        ent_new_ref[...] = moments(ent_pick, 0, ent_rows_ref[...])
-        rel_new_ref[...] = moments(rel_pick, 1, rel_rows_ref[...])
-        ent_col_ref[...] = ent_cols_ref[...]
-        rel_col_ref[...] = rel_cols_ref[...]
-        for i in range(2):
-            loss_out_ref[i] = loss_ref[0, i]
-
-    grad = sum(mm(part, ent_pick[...]) for part in two(ent_back_ref[...]))
-    ent_g_ref[...] = grad
-    new = ent_ref[...] - grad * lax.rsqrt(ent_new_ref[...]) * step_ref[:, 0:1]
-    ent_w_ref[...] = new
-    ent_c_ref[...] = new.astype(BF16)
-    grad = sum(mm(part, rel_pick[...]) for part in two(rel_back_ref[...]))
+    layers, width, _ = rel_s.shape
+    blocks = width // rows
+
+    def span_of(t):
+        return pl.ds(pl.multiple_of(t * rows, rows), rows)
+
+    def loads(t):
+        span = span_of(t)
+        return (
+            pltpu.make_async_copy(ent_ref.at[span], ent_s.at[span], load_sem.at[0, t]),
+            pltpu.make_async_copy(rel_ref.at[:, span], rel_s.at[:, span], load_sem.at[1, t]),
+        )
+
+    def stores(t):
+        span = span_of(t)
+        pairs = [
+            (ent_w.at[span], ent_w_ref.at[span]), (ent_c.at[span], ent_c_ref.at[span]),
+            (rel_w.at[:, span], rel_w_ref.at[:, span]), (rel_c.at[:, span], rel_c_ref.at[:, span]),
+        ]
+        return [pltpu.make_async_copy(a, b, store_sem.at[i, t]) for i, (a, b) in enumerate(pairs)]
+
+    def begin(t, carry):
+        for copy in loads(t):
+            copy.start()
+        return carry
+
+    lax.fori_loop(0, blocks, begin, 0)
+
+    def moments(pick, which, old):
+        hit = iota(pick.shape, 1) == ids_ref[:, which:which + 1]
+        pick[...] = jnp.where(hit, 1.0, 0.0).astype(BF16)
+        whole = jnp.max(jnp.where(hit, whole_ref[:, which:which + 1], 0.0), 0, keepdims=True)
+        return DECAY * old + (1.0 - DECAY) * (whole / width + EPS_SQ)
+
+    ent_new_ref[...] = moments(ent_pick, 0, ent_rows_ref[...])
+    ent_g[...] = sum(mm(part, ent_pick[...]) for part in two(ent_back_ref[...]))
+    grads = [pltpu.make_async_copy(ent_g, ent_g_ref, grad_sem.at[layers])]
+    grads[0].start()
+    rel_new_ref[...] = moments(rel_pick, 1, rel_rows_ref[...])
+    rel_g[...] = sum(mm(part, rel_pick[...]) for part in two(rel_back_ref[...]))
     for layer in range(layers):
-        rel_g_ref[layer] = grad
-        new = rel_ref[layer] - grad * lax.rsqrt(rel_new_ref[layer:layer + 1, :]) * step_ref[:, layer + 1:layer + 2]
-        rel_w_ref[layer] = new
-        rel_c_ref[layer] = new.astype(BF16)
+        grads.append(pltpu.make_async_copy(rel_g, rel_g_ref.at[layer], grad_sem.at[layer]))
+        grads[-1].start()
+    ent_col_ref[...] = ent_cols_ref[...]
+    rel_col_ref[...] = rel_cols_ref[...]
+    for i in range(2):
+        loss_out_ref[i] = loss_ref[0, i]
+    ent_root, rel_root = lax.rsqrt(ent_new_ref[...]), lax.rsqrt(rel_new_ref[...])
+
+    def block(t, carry):
+        span = span_of(t)
+        for copy in loads(t):
+            copy.wait()
+        new = ent_s[span, :] - ent_g[span, :] * ent_root * step_ref[span, 0:1]
+        ent_w[span, :] = new
+        ent_c[span, :] = new.astype(BF16)
+        grad = rel_g[span, :]
+        for layer in range(layers):
+            new = rel_s[layer, span, :] - grad * rel_root[layer:layer + 1, :] * step_ref[span, layer + 1:layer + 2]
+            rel_w[layer, span, :] = new
+            rel_c[layer, span, :] = new.astype(BF16)
+        for copy in stores(t):
+            copy.start()
+        return carry
+
+    lax.fori_loop(0, blocks, block, 0)
+
+    def end(t, carry):
+        for copy in stores(t):
+            copy.wait()
+        return carry
+
+    lax.fori_loop(0, blocks, end, 0)
+    for copy in grads:
+        copy.wait()
 
 
 def fused(
@@ -854,7 +918,7 @@
     ent_back, rel_back, ids, whole, ent_col, rel_col, steps, loss = pl.pallas_call(
         functools.partial(step_kernel, n_mp, cap, negatives, 32),
         out_shape=outs,
-        in_specs=[hbm, hbm] + [vmem] * (len(args) - 2),
+        in_specs=[hbm] * len(args),
         out_specs=[vmem] * len(outs),
         scratch_shapes=[
             V((width, owned), F32), V((layers, width, owned_rel), F32),
@@ -874,37 +938,34 @@
             V((n_mp, 16, LANES), F32), V((n_dp, 16, LANES), F32), V((8, LANES), F32),
             V((batches, 8, edges), F32), V((batches, 8, edges), F32),
             V((batches, 1, edges), F32), V((batches, 1, edges), F32),
-            sem((2,)), many, many, many, many, many, many, sem((2,)), sem((2,)),
+            sem((2 + len(args) - 2,)), many, many, many, many, many, many, sem((2,)), sem((2,)),
             many, many, sem((n_mp,)), sem((n_mp,)),
             many, many, many, many, sem((3,)), sem((3,)),
             sem((n_mp,)), sem((n_mp,)), sem((n_dp,)), sem((n_dp,)),
-        ],
+        ] + [V(a.shape, a.dtype) for a in args[2:]],
         compiler_params=pltpu.CompilerParams(
             collective_id=1, has_side_effects=True, vmem_limit_bytes=60 << 20
         ),
         name="step",
     )(*args)
     rows = 80 if width % 80 == 0 else width
-    ent_block = pl.BlockSpec((rows, owned), lambda i: (i, 0))
-    rel_block = pl.BlockSpec((layers, rows, owned_rel), lambda i: (0, i, 0))
-    slot_block = pl.BlockSpec((rows, slots), lambda i: (i, 0))
-    fixed = lambda a: pl.BlockSpec(a.shape, lambda i, n=a.ndim: (0,) * n)
     smem = pl.BlockSpec(memory_space=pltpu.SMEM)
     ent_rows, rel_rows = entity_rows[None], relation_rows
     small = (ent_rows, rel_rows, ent_col, rel_col)
     ent_w, ent_g, ent_c, rel_w, rel_g, rel_c, ent_new, rel_new, ent_col, rel_col, loss = pl.pallas_call(
-        update_kernel,
-        grid=(width // rows,),
+        functools.partial(update_kernel, rows),
         out_shape=[
             shape(ent_t.shape, F32), shape(ent_t.shape, F32), shape(ent_t.shape, BF16),
             shape(rel_t.shape, F32), shape(rel_t.shape, F32), shape(rel_t.shape, BF16),
         ] + [shape(a.shape, F32) for a in small] + [shape((2,), F32)],
-        in_specs=[
-            ent_block, rel_block, slot_block, slot_block, fixed(ids), fixed(whole), fixed(ent_rows), fixed(rel_rows),
-            pl.BlockSpec((rows, LANES), lambda i: (i, 0)), fixed(ent_col), fixed(rel_col), smem,
+        in_specs=[hbm, hbm] + [vmem] * 9 + [smem],
+        out_specs=[hbm] * 6 + [vmem] * 4 + [smem],
+        scratch_shapes=[
+            V((slots, owned), BF16), V((slots, owned_rel), BF16), V(ent_t.shape, F32), V(rel_t.shape, F32),
+            V(ent_t.shape, F32), V(ent_t.shape, F32), V(ent_t.shape, BF16),
+            V(rel_t.shape, F32), V(rel_t.shape[1:], F32), V(rel_t.shape, BF16),
+            sem((2, width // rows)), sem((4, width // rows)), sem((layers + 1,)),
         ],
-        out_specs=[ent_block] * 3 + [rel_block] * 3 + [fixed(a) for a in small] + [smem],
-        scratch_shapes=[V((slots, owned), BF16), V((slots, owned_rel), BF16)],
         compiler_params=pltpu.CompilerParams(vmem_limit_bytes=60 << 20),
         name="update",
     )(ent_t, rel_t, ent_back, rel_back, ids, whole, ent_rows, rel_rows, steps, ent_col, rel_col, loss)

time: 111 us -> 108 us (0.973)
  Pallas kernels: 110 us -> 107 us
    pallas_call x1, Pallas kernels: 10.7 us -> 9.3 us  [fused(): pl.pallas_call(functools.partial(update_kernel, rows), out_shape=[shape(e...]
    pallas_call x1, Pallas kernels: 99 us -> 97.7 us  [fused(): pl.pallas_call(functools.partial(step_kernel, n_mp, cap, negatives, 32),...]
where the time goes in v1:
time: 108 us
  Pallas kernels  107 us (99%)
    pallas_call x1, Pallas kernels, fused(): pl.pallas_call(functools.partial(step_kernel, n_mp, cap, negatives, 32),...  97.7 us
    pallas_call x1, Pallas kernels, fused(): pl.pallas_call(functools.partial(update_kernel, rows), out_shape=[shape(e...  9.3 us

profile of v1, /device:TPU:0, one launch (start us, length us, event | category | flops | bytes accessed | tf_op | source)
XLA Modules:
  0.0 107.8 jit_solution(6535734039310504885)
XLA Ops:
  0.6 97.7 %step.1 = (f32[400,256]{1,0:T(8,128)}, f32[400,256]{1,0:T(8,128)}, s32[256,128]{1,0:T(8,128)}, f32[256,128]{1,0:T(8,128)}, f32[1,400]{1,0:T(1,128)}, /*index=5*/...) custom-call(f32[400,2048]{1,0:T(8,128)} %bitcast.12, f32[2,400,784]{2,1,0:T(8,128)} %bitcast.14, ...), custom_call_target="tpu_custom_call" | custom-call | tf_op jit(solution)/shard_map/step/pallas_call | solution.py:918
  98.3 9.3 %update.1 = (f32[400,2048]{1,0:T(8,128)}, f32[400,2048]{1,0:T(8,128)}, bf16[400,2048]{1,0:T(8,128)(2,1)}, f32[2,400,784]{2,1,0:T(8,128)}, f32[2,400,784]{2,1,0:T...) custom-call(f32[400,2048]{1,0:T(8,128)} %bitcast.13, ...), custom_call_target="tpu_custom_call" | custom-call | tf_op jit(solution)/shard_map/update/pallas_call | solution.py:955

commit v2 on v1

--- a/solution.py
+++ b/solution.py
@@ -306,11 +306,18 @@
 
         lax.fori_loop(1, self.devices, step, 0)
 
+    def each_sender(self, act):
+        def step(i, carry):
+            act(lax.rem(self.me + self.devices - i, self.devices))
+            return carry
+
+        lax.fori_loop(1, self.devices, step, 0)
+
     def start(self):
         self.each(lambda p: self.copy(p, self.me).start())
 
     def arrived(self):
-        self.each(lambda p: self.copy(p, p).wait_recv())
+        self.each_sender(lambda p: self.copy(p, p).wait_recv())
 
     def left(self):
         self.each(lambda p: self.copy(p, self.me).wait_send())
@@ -474,7 +481,7 @@
         give_ent.copy(p, p).wait_recv()
         forward(p).start()
 
-    give_ent.each(pass_on)
+    give_ent.each_sender(pass_on)
 
     def hand(i, src, dst):
         return pltpu.make_async_remote_copy(
@@ -713,9 +720,18 @@
             sums.append(k + jnp.sum(moment * share_of, 0, keepdims=True))
         return whole, out, sums
 
+    for copy in [to_mate, onward, through, over_x, direct] + count_copies:
+        copy.wait_send()
+
+    def gone(p, carry):
+        forward(p).wait_send()
+        return carry
+
+    lax.fori_loop(0, devices, gone, 0)
     back_rel.arrived()
     rel_back = unpack(back_in_rel, tail_s.at[1]) * scale
     rel_whole, more_rows, more_sums = row_sums(rel_back, *rel_same)
+    back_rel.left()
     back_ent.arrived()
     ent_back = unpack(back_in_ent, tail_s.at[0]) * scale
     ent_whole, rows, sums = row_sums(ent_back, *ent_same)
@@ -750,21 +766,9 @@
         lane = iota(whole_ref.shape, 1)
         whole_ref[...] = jnp.where(lane == 0, ent_whole, jnp.where(lane == 1, rel_whole, 0.0))
 
-    def settle():
-        for copy in [to_mate, onward, through, over_x, direct] + count_copies:
-            copy.wait_send()
-
-        def gone(p, carry):
-            forward(p).wait_send()
-            return carry
-
-        lax.fori_loop(0, devices, gone, 0)
-        back_rel.left()
-        back_ent.left()
-
     copies = share("mp", n_mp, mp, part_mp, sum_mp_send, sum_mp_recv, write_out)
     part_dp[dp] = jnp.sum(part_mp[...], 0)
-    copies += share("dp", n_dp, dp, part_dp, sum_dp_send, sum_dp_recv, settle)
+    copies += share("dp", n_dp, dp, part_dp, sum_dp_send, sum_dp_recv, back_ent.left)
     total = jnp.sum(part_dp[...], 0)
     last = total[len(lines):len(lines) + 1, :]
     summed = [

time: 108 us -> 108 us (level)
  no operation moved by 1% of the time
where the time goes in v2:
time: 108 us
  Pallas kernels  107 us (99%)
    pallas_call x1, Pallas kernels, fused(): pl.pallas_call(functools.partial(step_kernel, n_mp, cap, negatives, 32),...  97.6 us
    pallas_call x1, Pallas kernels, fused(): pl.pallas_call(functools.partial(update_kernel, rows), out_shape=[shape(e...  9.3 us

profile of v2, /device:TPU:0, one launch (start us, length us, event | category | flops | bytes accessed | tf_op | source)
XLA Modules:
  0.0 107.7 jit_solution(238944171657615647)
XLA Ops:
  0.6 97.6 %step.1 = (f32[400,256]{1,0:T(8,128)}, f32[400,256]{1,0:T(8,128)}, s32[256,128]{1,0:T(8,128)}, f32[256,128]{1,0:T(8,128)}, f32[1,400]{1,0:T(1,128)}, /*index=5*/...) custom-call(f32[400,2048]{1,0:T(8,128)} %bitcast.12, f32[2,400,784]{2,1,0:T(8,128)} %bitcast.14, ...), custom_call_target="tpu_custom_call" | custom-call | tf_op jit(solution)/shard_map/step/pallas_call | solution.py:922
  98.2 9.3 %update.1 = (f32[400,2048]{1,0:T(8,128)}, f32[400,2048]{1,0:T(8,128)}, bf16[400,2048]{1,0:T(8,128)(2,1)}, f32[2,400,784]{2,1,0:T(8,128)}, f32[2,400,784]{2,1,0:T...) custom-call(f32[400,2048]{1,0:T(8,128)} %bitcast.13, ...), custom_call_target="tpu_custom_call" | custom-call | tf_op jit(solution)/shard_map/update/pallas_call | solution.py:959
